TPU v7x, 32 devices: a whole 2x2x4 slice. The times are simulated.
32 devices in a mesh: ctx: 8 (over y, x, core), seq: 4 (over z).
Axes of the slice: x: 2, y: 2, z: 4, core: 2. Of those that a mesh axis runs over, the one named last changes fastest.
Arguments:
- queries: bfloat16 [4096, 4096], P(('seq', 'ctx')), may hold values from -6 to 6
- key_proj: bfloat16 [4096, 4096], P(('seq', 'ctx')), may hold values from -6 to 6
- value_proj: bfloat16 [4096, 4096], P(('seq', 'ctx')), may hold values from -6 to 6
- decay_rate: float32 [16, 4096], P(None, 'ctx'), may hold values from 2.4414063e-05 to 0.06
- residue: float32 [16, 4096], P(None, 'ctx'), may hold values from -1 to 1
- skip_gain: float32 [4096], P('ctx'), may hold values from -1 to 1
Outputs:
- operator_out: bfloat16 [4096, 4096], P(('seq', 'ctx'))
All inputs are finite; a program needn't handle non-finite values.
Results may differ from a plain program's by a relative error of at most 0.011.
Values may be sent and summed in bfloat16 or wider, within the bound.
A program may use at most 320 MiB of HBM per device.

v0:
```python
import functools

import jax
import jax.numpy as jnp
from jax import lax
from jax.experimental import pallas as pl
from jax.experimental.pallas import tpu as pltpu
from jax.sharding import PartitionSpec as P

LANES = 128
BLOCKS = 8
MESH = pl.DeviceIdType.MESH


def kernel(
    nctx, nseq, modes, par_in, q_hbm, k_hbm, v_hbm, out_hbm,
    par, kbuf, vbuf, qbuf, obuf, mixed, inner, carry, pows, state_out, state_in, local_start,
    totals, start_out, start_in, turned,
    k_sem, v_sem, q_sem, o_sem, par_send, par_recv, st_send, st_recv, tot_send, tot_recv,
    go_send, go_recv,
):
    ctx, seq = lax.axis_index("ctx"), lax.axis_index("seq")
    tokens, width = kbuf.shape[1], kbuf.shape[2]
    groups = width // LANES
    steps = tokens // BLOCKS

    def slot(i):
        return lax.rem(ctx + i, nctx)

    def columns(c):
        return pl.ds(pl.multiple_of(c * width, LANES), width)

    def fetch(hbm, buf, sem, c):
        return pltpu.make_async_copy(hbm.at[:, columns(c)], buf.at[c], sem.at[c])

    def store_out(c):
        return pltpu.make_async_copy(obuf.at[c], out_hbm.at[:, columns(c)], o_sem.at[c])

    def swap(src, dst, to, send, recv, axis, other):
        return pltpu.make_async_remote_copy(
            src_ref=src, dst_ref=dst.at[to], send_sem=send.at[other], recv_sem=recv.at[to],
            device_id={axis: other}, device_id_type=MESH)

    def par_copy(c, to):
        return swap(par_in, par, to, par_send, par_recv, "ctx", c)

    def state_copy(c, to):
        return swap(state_out.at[c], state_in, to, st_send, st_recv, "ctx", c)

    def total_copy(s, to):
        return swap(totals.at[seq], totals, to, tot_send, tot_recv, "seq", s)

    def start_copy(c, to):
        return swap(start_out.at[c], start_in, to, go_send, go_recv, "ctx", c)

    def each(count, body):
        lax.fori_loop(0, count, lambda i, x: (body(i), x)[1], 0)

    @functools.partial(each, nctx)
    def _(i):
        fetch(k_hbm, kbuf, k_sem, slot(i)).start()
        fetch(v_hbm, vbuf, v_sem, slot(i)).start()

    barrier = pltpu.get_barrier_semaphore()

    @functools.partial(each, nctx - 1)
    def _(i):
        pl.semaphore_signal(barrier, inc=1, device_id={"ctx": slot(i + 1)}, device_id_type=MESH)

    @functools.partial(each, nseq - 1)
    def _(i):
        pl.semaphore_signal(
            barrier, inc=1, device_id={"seq": lax.rem(seq + i + 1, nseq)}, device_id_type=MESH)

    pl.semaphore_wait(barrier, nctx + nseq - 2)

    @functools.partial(each, nctx - 1)
    def _(i):
        par_copy(slot(i + 1), ctx).start()

    par[ctx] = par_in[...]

    @functools.partial(each, nctx)
    def _(i):
        fetch(q_hbm, qbuf, q_sem, slot(i)).start()

    block = lax.broadcasted_iota(jnp.int32, (BLOCKS, LANES), 0)

    def lanes(j):
        return pl.ds(pl.multiple_of(j * LANES, LANES), LANES)

    def wide(row):
        return jnp.broadcast_to(row, (BLOCKS, LANES))

    @functools.partial(each, nctx)
    def _(i):
        c = slot(i)

        @pl.when(i > 0)
        def _():
            par_copy(c, c).wait_recv()

        fetch(k_hbm, kbuf, k_sem, c).wait()
        fetch(v_hbm, vbuf, v_sem, c).wait()

        @functools.partial(each, groups)
        def _(j):
            g = c * groups + j
            product = kbuf[c, :, lanes(j)].astype(jnp.float32) * vbuf[c, :, lanes(j)].astype(jnp.float32)
            mixed[g] = product.astype(jnp.bfloat16).astype(jnp.float32)
            rate = par[c, 0:modes, lanes(j)]
            pows[g, 0:modes, :] = jnp.exp(-rate)
            pows[g, modes:2 * modes, :] = jnp.exp(-steps * rate)
            x = [mixed[g, pl.ds(a, BLOCKS, stride=steps), :] for a in range(steps)]
            for m in range(modes):
                p = wide(pows[g, pl.ds(m, 1), :])
                span = wide(pows[g, pl.ds(modes + m, 1), :])
                state = x[0]
                for a in range(1, steps):
                    state = state * p + x[a]
                shift = 1
                while shift < BLOCKS:
                    moved = pltpu.roll(state, shift, 0)
                    state = state + jnp.where(block >= shift, span, 0.0) * moved
                    span = span * span
                    shift *= 2
                carry[g, m] = jnp.where(block >= 1, pltpu.roll(state, 1, 0), 0.0)
                state_out[c, pl.ds(m, 1), lanes(j)] = state[BLOCKS - 1:, :]

        @pl.when(i > 0)
        def _():
            state_copy(c, ctx).start()

    def inside(first, last):
        def one(i):
            c = slot(i)

            @functools.partial(each, groups)
            def _(j):
                g = c * groups + j
                p = pows[g, 0:modes, :]
                w = par[c, modes:2 * modes, lanes(j)]
                gain = par[c, pl.ds(2 * modes, 1), lanes(j)]
                taps = []
                for a in range(steps):
                    tap = jnp.sum(w, axis=0, keepdims=True)
                    taps.append(wide(tap + gain if a == 0 else tap))
                    w = w * p
                x = [mixed[g, pl.ds(a, BLOCKS, stride=steps), :] for a in range(steps)]
                for a in range(steps):
                    y = taps[0] * x[a]
                    for b in range(a):
                        y = y + taps[a - b] * x[b]
                    inner[g, a] = y

        lax.fori_loop(first, last, lambda i, x: (one(i), x)[1], 0)

    cut = [0, (nctx * 3) // 8, (nctx * 6) // 8, nctx]
    inside(cut[0], cut[1])

    state_in[ctx] = state_out[ctx]

    @functools.partial(each, nctx - 1)
    def _(i):
        state_copy(slot(i + 1), slot(i + 1)).wait_recv()

    rate = par_in[0:modes, :]
    decay = jnp.exp(-tokens * rate)

    def link(s, state):
        local_start[s] = state
        return state * decay + state_in[s]

    totals[seq] = lax.fori_loop(0, nctx, link, jnp.zeros_like(rate))

    @functools.partial(each, nseq - 1)
    def _(i):
        total_copy(lax.rem(seq + i + 1, nseq), seq).start()

    inside(cut[1], cut[2])

    @functools.partial(each, nseq - 1)
    def _(i):
        s = lax.rem(seq + i + 1, nseq)
        total_copy(s, s).wait_recv()

    span_decay = jnp.exp(-(tokens * nctx) * rate)
    begin = lax.fori_loop(
        0, seq, lambda s, state: state * span_decay + totals[s], jnp.zeros_like(rate))

    @functools.partial(each, nctx)
    def _(i):
        c = slot(i)
        reach = jnp.exp(-(tokens * c).astype(jnp.float32) * rate)
        start_out[c] = local_start[c] + reach * begin

        @pl.when(i > 0)
        def _():
            start_copy(c, ctx).start()

    start_in[ctx] = start_out[ctx]
    inside(cut[2], cut[3])

    far = -steps * block.astype(jnp.float32)

    @functools.partial(each, nctx)
    def _(i):
        c = slot(i)

        @pl.when(i > 0)
        def _():
            start_copy(c, c).wait_recv()

        fetch(q_hbm, qbuf, q_sem, c).wait()

        @functools.partial(each, groups)
        def _(j):
            g = c * groups + j
            y = [inner[g, a] for a in range(steps)]
            for m in range(modes):
                p = wide(pows[g, pl.ds(m, 1), :])
                rate_m = wide(par[c, pl.ds(m, 1), lanes(j)])
                w = wide(par[c, pl.ds(modes + m, 1), lanes(j)])
                start = wide(start_in[c, pl.ds(m, 1), lanes(j)])
                lifted = (carry[g, m] + jnp.exp(far * rate_m) * start) * (w * p)
                for a in range(steps):
                    y[a] = y[a] + lifted
                    if a < steps - 1:
                        lifted = lifted * p
            for a in range(steps):
                turned[pl.ds(a, BLOCKS, stride=steps), :] = y[a]
            pre = turned[...].astype(jnp.bfloat16).astype(jnp.float32)
            gated = qbuf[c, :, lanes(j)].astype(jnp.float32) * pre
            obuf[c, :, lanes(j)] = gated.astype(jnp.bfloat16)

        store_out(c).start()

    @functools.partial(each, nctx)
    def _(i):
        store_out(slot(i)).wait()

    @functools.partial(each, nctx - 1)
    def _(i):
        c = slot(i + 1)
        par_copy(c, ctx).wait_send()
        state_copy(c, ctx).wait_send()
        start_copy(c, ctx).wait_send()

    @functools.partial(each, nseq - 1)
    def _(i):
        total_copy(lax.rem(seq + i + 1, nseq), seq).wait_send()


def local(nctx, nseq, queries, key_proj, value_proj, decay_rate, residue, skip_gain):
    modes, width = decay_rate.shape
    tokens, channels = queries.shape
    groups = channels // LANES
    weight = residue * jnp.sqrt(-jnp.expm1(-2.0 * decay_rate))
    rows = -(-(2 * modes + 1) // 8) * 8
    par = jnp.concatenate(
        [decay_rate, weight, jnp.broadcast_to(skip_gain[None], (rows - 2 * modes, width))], axis=0)
    f32, bf16 = jnp.float32, jnp.bfloat16
    any_spec = pl.BlockSpec(memory_space=pl.ANY)
    piece = pltpu.VMEM((nctx, tokens, width), bf16)
    state = pltpu.VMEM((nctx, modes, width), f32)
    sems = [pltpu.SemaphoreType.DMA((nctx,))] * 4 + [
        pltpu.SemaphoreType.DMA((n,)) for n in (nctx, nctx, nctx, nctx, nseq, nseq, nctx, nctx)]
    return pl.pallas_call(
        functools.partial(kernel, nctx, nseq, modes),
        out_shape=jax.ShapeDtypeStruct((tokens, channels), bf16),
        in_specs=[pl.BlockSpec(memory_space=pltpu.VMEM)] + [any_spec] * 3,
        out_specs=any_spec,
        scratch_shapes=[
            pltpu.VMEM((nctx, rows, width), f32),
            piece, piece, piece, piece,
            pltpu.VMEM((groups, tokens, LANES), f32),
            pltpu.VMEM((groups, tokens // BLOCKS, BLOCKS, LANES), f32),
            pltpu.VMEM((groups, modes, BLOCKS, LANES), f32),
            pltpu.VMEM((groups, 2 * modes, LANES), f32),
            state, state, state,
            pltpu.VMEM((nseq, modes, width), f32),
            state, state,
            pltpu.VMEM((tokens, LANES), f32),
        ] + sems,
        compiler_params=pltpu.CompilerParams(
            collective_id=0, has_side_effects=True, vmem_limit_bytes=48 * 1024 * 1024),
        cost_estimate=pl.CostEstimate(
            flops=tokens * channels * 90, bytes_accessed=8 * tokens * channels,
            transcendentals=groups * modes * LANES * 12),
    )(par, queries, key_proj, value_proj)


def solution(mesh):
    in_specs = (
        P(("seq", "ctx"), None),
        P(("seq", "ctx"), None),
        P(("seq", "ctx"), None),
        P(None, "ctx"),
        P(None, "ctx"),
        P("ctx"),
    )
    body = functools.partial(local, mesh.shape["ctx"], mesh.shape["seq"])
    return jax.shard_map(
        body, mesh=mesh, in_specs=in_specs, out_specs=P(("seq", "ctx"), None), check_vma=False)
```

profile of v0, /device:TPU:0, one launch (start us, length us, event | category | flops | bytes accessed | tf_op | source)
XLA Modules:
  0.0 39.0 jit_solution(16104218399191256854)
XLA Ops:
  0.0 0.7 %broadcast_in_dim.2 = f32[8,512]{1,0:T(8,128)S(1)} broadcast(f32[512]{0:T(512)} %param.11), dimensions={1} | broadcast | bytes 18432 | tf_op jit(solution)/shard_map/broadcast_in_dim | solution.py:261
  0.7 0.0 copy-start.3
  0.7 0.9 %sqrt_multiply_fusion = f32[16,512]{1,0:T(8,128)S(1)} fusion(f32[16,512]{1,0:T(8,128)} %param.10, f32[16,512]{1,0:T(8,128)} %param.9), kind=kLoop, calls=%fused_computation.1 | loop fusion | flops 24576 | bytes 98304 | tf_op jit(solution)/shard_map/mul | solution.py:258
  1.5 0.0 copy-done.3
  1.6 0.0 copy-start
  1.6 1.2 %copy-done = bf16[128,4096]{1,0:T(8,128)(2,1)S(1)} copy-done((bf16[128,4096]{1,0:T(8,128)(2,1)S(1)}, bf16[128,4096]{1,0:T(8,128)(2,1)}, u32[]{:S(2)}) %copy-start) | copy-done | bytes 1048600
  2.8 0.0 copy-start.1
  2.8 1.2 %copy-done.1 = bf16[128,4096]{1,0:T(8,128)(2,1)S(1)} copy-done((bf16[128,4096]{1,0:T(8,128)(2,1)S(1)}, bf16[128,4096]{1,0:T(8,128)(2,1)}, u32[]{:S(2)}) %copy-start.1) | copy-done | bytes 1048600
  4.0 0.0 copy-start.2
  4.0 1.2 %copy-done.2 = bf16[128,4096]{1,0:T(8,128)(2,1)S(1)} copy-done((bf16[128,4096]{1,0:T(8,128)(2,1)S(1)}, bf16[128,4096]{1,0:T(8,128)(2,1)}, u32[]{:S(2)}) %copy-start.2) | copy-done | bytes 1048600
  5.3 32.7 %shard_map.64 = bf16[128,4096]{1,0:T(8,128)(2,1)S(1)} custom-call(f32[40,512]{1,0:T(8,128)S(1)} %pad_maximum_fusion.par_in, bf16[128,4096]{1,0:T(8,128)(2,1)S(1)} %copy-done, bf16[128,4096]{1,0:T(8,128)(2,1)S(1)} %copy-done.1, bf16[128,4096]{1,0:T(8,128)(2,1)S(1)} %copy-done.2), custom_call_target="tpu_custom_call" | custom-call | flops 47185920 | bytes 4194304 | tf_op jit(solution)/shard_map/pallas_call | solution.py:268
  38.0 1.0 %copy.8 = bf16[128,4096]{1,0:T(8,128)(2,1)} copy(bf16[128,4096]{1,0:T(8,128)(2,1)S(1)} %shard_map.64) | data formatting | bytes 2097152
  (1 shorter events, 0.0 us)
Async XLA Ops:
  0.7 0.9 %copy-start.3 = (f32[16,512]{1,0:T(8,128)S(1)}, f32[16,512]{1,0:T(8,128)}, u32[]{:S(2)}) copy-start(f32[16,512]{1,0:T(8,128)} %param.9) | copy-start | bytes 98308
  1.6 1.2 %copy-start = (bf16[128,4096]{1,0:T(8,128)(2,1)S(1)}, bf16[128,4096]{1,0:T(8,128)(2,1)}, u32[]{:S(2)}) copy-start(bf16[128,4096]{1,0:T(8,128)(2,1)} %q_hbm.1) | copy-start | bytes 3145732
  2.8 1.2 %copy-start.1 = (bf16[128,4096]{1,0:T(8,128)(2,1)S(1)}, bf16[128,4096]{1,0:T(8,128)(2,1)}, u32[]{:S(2)}) copy-start(bf16[128,4096]{1,0:T(8,128)(2,1)} %k_hbm.1) | copy-start | bytes 3145732
  4.0 1.2 %copy-start.2 = (bf16[128,4096]{1,0:T(8,128)(2,1)S(1)}, bf16[128,4096]{1,0:T(8,128)(2,1)}, u32[]{:S(2)}) copy-start(bf16[128,4096]{1,0:T(8,128)(2,1)} %v_hbm.1) | copy-start | bytes 3145732
where the time goes:
time: 39.5 us; the launch traced here: 39 us
  Pallas kernels  32.7 us (83%)
  local copies, waits for them, and re-layouts  5.33 us (13%)
  other arithmetic  0.87 us (2%)
    pallas_call x1, Pallas kernels, local(): pl.pallas_call(functools.partial(kernel, nctx, nseq, modes), out_shape=ja...  32.7 us
    unnamed x9, local copies, waits for them, and re-layouts  4.64 us
    mul x1, other arithmetic, local(): weight = residue * jnp.sqrt(-jnp.expm1(-2.0 * decay_rate))  0.86 us

commit v1 on v0

--- a/solution.py
+++ b/solution.py
@@ -12,11 +12,18 @@
 MESH = pl.DeviceIdType.MESH
 
 
+def minus_expm1(x):
+    series = jnp.ones_like(x)
+    for n in range(9, 1, -1):
+        series = 1.0 - series * x * (1.0 / n)
+    return jnp.where(x < 0.25, x * series, 1.0 - jnp.exp(-x))
+
+
 def kernel(
-    nctx, nseq, modes, par_in, q_hbm, k_hbm, v_hbm, out_hbm,
-    par, kbuf, vbuf, qbuf, obuf, mixed, inner, carry, pows, state_out, state_in, local_start,
+    nctx, nseq, modes, rate_in, residue_in, gain_in, q_hbm, k_hbm, v_hbm, out_hbm,
+    rates, lifts, lift_out, kbuf, vbuf, qbuf, obuf, mixed, inner, carry, pows, state_out, state_in, local_start,
     totals, start_out, start_in, turned,
-    k_sem, v_sem, q_sem, o_sem, par_send, par_recv, st_send, st_recv, tot_send, tot_recv,
+    k_sem, v_sem, q_sem, o_sem, rate_send, rate_recv, lift_send, lift_recv, st_send, st_recv, tot_send, tot_recv,
     go_send, go_recv,
 ):
     ctx, seq = lax.axis_index("ctx"), lax.axis_index("seq")
@@ -41,8 +48,11 @@
             src_ref=src, dst_ref=dst.at[to], send_sem=send.at[other], recv_sem=recv.at[to],
             device_id={axis: other}, device_id_type=MESH)
 
-    def par_copy(c, to):
-        return swap(par_in, par, to, par_send, par_recv, "ctx", c)
+    def rate_copy(c, to):
+        return swap(rate_in, rates, to, rate_send, rate_recv, "ctx", c)
+
+    def lift_copy(c, to):
+        return swap(lift_out, lifts, to, lift_send, lift_recv, "ctx", c)
 
     def state_copy(c, to):
         return swap(state_out.at[c], state_in, to, st_send, st_recv, "ctx", c)
@@ -76,9 +86,17 @@
 
     @functools.partial(each, nctx - 1)
     def _(i):
-        par_copy(slot(i + 1), ctx).start()
-
-    par[ctx] = par_in[...]
+        rate_copy(slot(i + 1), ctx).start()
+
+    rate = rate_in[...]
+    rates[ctx] = rate
+    lift_out[0:modes, :] = residue_in[...] * jnp.sqrt(minus_expm1(2.0 * rate))
+    lift_out[modes:, :] = jnp.broadcast_to(gain_in[...], (lift_out.shape[0] - modes, width))
+    lifts[ctx] = lift_out[...]
+
+    @functools.partial(each, nctx - 1)
+    def _(i):
+        lift_copy(slot(i + 1), ctx).start()
 
     @functools.partial(each, nctx)
     def _(i):
@@ -98,7 +116,7 @@
 
         @pl.when(i > 0)
         def _():
-            par_copy(c, c).wait_recv()
+            rate_copy(c, c).wait_recv()
 
         fetch(k_hbm, kbuf, k_sem, c).wait()
         fetch(v_hbm, vbuf, v_sem, c).wait()
@@ -108,7 +126,7 @@
             g = c * groups + j
             product = kbuf[c, :, lanes(j)].astype(jnp.float32) * vbuf[c, :, lanes(j)].astype(jnp.float32)
             mixed[g] = product.astype(jnp.bfloat16).astype(jnp.float32)
-            rate = par[c, 0:modes, lanes(j)]
+            rate = rates[c, :, lanes(j)]
             pows[g, 0:modes, :] = jnp.exp(-rate)
             pows[g, modes:2 * modes, :] = jnp.exp(-steps * rate)
             x = [mixed[g, pl.ds(a, BLOCKS, stride=steps), :] for a in range(steps)]
@@ -135,12 +153,16 @@
         def one(i):
             c = slot(i)
 
+            @pl.when(i > 0)
+            def _():
+                lift_copy(c, c).wait_recv()
+
             @functools.partial(each, groups)
             def _(j):
                 g = c * groups + j
                 p = pows[g, 0:modes, :]
-                w = par[c, modes:2 * modes, lanes(j)]
-                gain = par[c, pl.ds(2 * modes, 1), lanes(j)]
+                w = lifts[c, 0:modes, lanes(j)]
+                gain = lifts[c, pl.ds(modes, 1), lanes(j)]
                 taps = []
                 for a in range(steps):
                     tap = jnp.sum(w, axis=0, keepdims=True)
@@ -164,7 +186,6 @@
     def _(i):
         state_copy(slot(i + 1), slot(i + 1)).wait_recv()
 
-    rate = par_in[0:modes, :]
     decay = jnp.exp(-tokens * rate)
 
     def link(s, state):
@@ -219,8 +240,8 @@
             y = [inner[g, a] for a in range(steps)]
             for m in range(modes):
                 p = wide(pows[g, pl.ds(m, 1), :])
-                rate_m = wide(par[c, pl.ds(m, 1), lanes(j)])
-                w = wide(par[c, pl.ds(modes + m, 1), lanes(j)])
+                rate_m = wide(rates[c, pl.ds(m, 1), lanes(j)])
+                w = wide(lifts[c, pl.ds(m, 1), lanes(j)])
                 start = wide(start_in[c, pl.ds(m, 1), lanes(j)])
                 lifted = (carry[g, m] + jnp.exp(far * rate_m) * start) * (w * p)
                 for a in range(steps):
@@ -242,7 +263,8 @@
     @functools.partial(each, nctx - 1)
     def _(i):
         c = slot(i + 1)
-        par_copy(c, ctx).wait_send()
+        rate_copy(c, ctx).wait_send()
+        lift_copy(c, ctx).wait_send()
         state_copy(c, ctx).wait_send()
         start_copy(c, ctx).wait_send()
 
@@ -255,23 +277,22 @@
     modes, width = decay_rate.shape
     tokens, channels = queries.shape
     groups = channels // LANES
-    weight = residue * jnp.sqrt(-jnp.expm1(-2.0 * decay_rate))
-    rows = -(-(2 * modes + 1) // 8) * 8
-    par = jnp.concatenate(
-        [decay_rate, weight, jnp.broadcast_to(skip_gain[None], (rows - 2 * modes, width))], axis=0)
+    rows = -(-(modes + 1) // 8) * 8
     f32, bf16 = jnp.float32, jnp.bfloat16
-    any_spec = pl.BlockSpec(memory_space=pl.ANY)
+    any_spec = pl.BlockSpec(memory_space=pltpu.HBM)
     piece = pltpu.VMEM((nctx, tokens, width), bf16)
     state = pltpu.VMEM((nctx, modes, width), f32)
     sems = [pltpu.SemaphoreType.DMA((nctx,))] * 4 + [
-        pltpu.SemaphoreType.DMA((n,)) for n in (nctx, nctx, nctx, nctx, nseq, nseq, nctx, nctx)]
+        pltpu.SemaphoreType.DMA((n,)) for n in (nctx, nctx, nctx, nctx, nctx, nctx, nseq, nseq, nctx, nctx)]
     return pl.pallas_call(
         functools.partial(kernel, nctx, nseq, modes),
         out_shape=jax.ShapeDtypeStruct((tokens, channels), bf16),
-        in_specs=[pl.BlockSpec(memory_space=pltpu.VMEM)] + [any_spec] * 3,
+        in_specs=[pl.BlockSpec(memory_space=pltpu.VMEM)] * 3 + [any_spec] * 3,
         out_specs=any_spec,
         scratch_shapes=[
+            state,
             pltpu.VMEM((nctx, rows, width), f32),
+            pltpu.VMEM((rows, width), f32),
             piece, piece, piece, piece,
             pltpu.VMEM((groups, tokens, LANES), f32),
             pltpu.VMEM((groups, tokens // BLOCKS, BLOCKS, LANES), f32),
@@ -283,11 +304,11 @@
             pltpu.VMEM((tokens, LANES), f32),
         ] + sems,
         compiler_params=pltpu.CompilerParams(
-            collective_id=0, has_side_effects=True, vmem_limit_bytes=48 * 1024 * 1024),
+            collective_id=0, has_side_effects=True, vmem_limit_bytes=60 * 1024 * 1024),
         cost_estimate=pl.CostEstimate(
             flops=tokens * channels * 90, bytes_accessed=8 * tokens * channels,
             transcendentals=groups * modes * LANES * 12),
-    )(par, queries, key_proj, value_proj)
+    )(decay_rate, residue, skip_gain[None], queries, key_proj, value_proj)
 
 
 def solution(mesh):

time: 39.5 us -> 34 us (0.86)
  local copies, waits for them, and re-layouts: 5.33 us -> 2.29 us
  Pallas kernels: 32.7 us -> 31.3 us
  other arithmetic: 0.87 us -> 0 us
    unnamed x9 -> x1, local copies, waits for them, and re-layouts: 4.64 us -> 2.29 us
    pallas_call x1, Pallas kernels: 32.7 us -> 31.3 us  [local(): pl.pallas_call(functools.partial(kernel, nctx, nseq, modes), out_shape=ja...]
    mul x1 -> x0, other arithmetic: 0.86 us -> none  [local(): weight = residue * jnp.sqrt(-jnp.expm1(-2.0 * decay_rate))]
    broadcast_in_dim x1 -> x0, local copies, waits for them, and re-layouts: 0.68 us -> none  [local(): jnp.broadcast_to(skip_gain[None], (rows - 2 * modes, width))]
where the time goes in v1:
time: 34 us; the launch traced here: 33.6 us
  Pallas kernels  31.3 us (92%)
  local copies, waits for them, and re-layouts  2.29 us (7%)
    pallas_call x1, Pallas kernels, local(): pl.pallas_call(functools.partial(kernel, nctx, nseq, modes), out_shape=ja...  31.3 us
    unnamed x1, local copies, waits for them, and re-layouts  2.29 us

profile of v1, /device:TPU:0, one launch (start us, length us, event | category | flops | bytes accessed | tf_op | source)
XLA Modules:
  0.0 33.6 jit_solution(16963973495302071574)
XLA Ops:
  0.0 31.3 %shard_map.64 = bf16[128,4096]{1,0:T(8,128)(2,1)} custom-call(f32[16,512]{1,0:T(8,128)} %rate_in.1, f32[16,512]{1,0:T(8,128)} %residue_in.1, f32[1,512]{1,0:T(1,128)} %bitcast.1, bf16[128,4096]{1,0:T(8,128)(2,1)} %q_hbm.1, bf16[128,4096]{1,0:T(8,128)(2,1)} %k_hbm.1, bf16[128,4096]{1,0:T(8,128)(2,1)} %v_hbm.1), custom_call_target="tpu_custom_call" | custom-call | flops 47185920 | bytes 4194304 | tf_op jit(solution)/shard_map/pallas_call | solution.py:287
  31.3 2.3 %copy.8 = bf16[128,4096]{1,0:T(8,128)(2,1)} copy(bf16[128,4096]{1,0:T(8,128)(2,1)} %shard_map.64) | data formatting | bytes 2097152

commit v2 on v1

v2 whole, which is shorter than its diff:
```python
import functools

import jax
import jax.numpy as jnp
from jax import lax
from jax.experimental import pallas as pl
from jax.experimental.pallas import tpu as pltpu
from jax.sharding import PartitionSpec as P

LANES = 128
BLOCKS = 8
MESH = pl.DeviceIdType.MESH


def minus_expm1(x):
    series = jnp.ones_like(x)
    for n in range(9, 1, -1):
        series = 1.0 - series * x * (1.0 / n)
    return jnp.where(x < 0.25, x * series, 1.0 - jnp.exp(-x))


def kernel(
    nctx, nseq, modes, halves, rate_in, residue_in, gain_in, q_hbm, k_hbm, v_hbm, out_hbm,
    rates, lifts, lift_out, kbuf, vbuf, qbuf, obuf, mixed, inner, carry, pows, state_out, state_in, local_start,
    totals, start_out, start_in, turned,
    k_sem, v_sem, q_sem, o_sem, rate_send, rate_recv, lift_send, lift_recv, st_send, st_recv, tot_send, tot_recv,
    go_send, go_recv,
):
    ctx, seq = lax.axis_index("ctx"), lax.axis_index("seq")
    tokens, width = kbuf.shape[1], kbuf.shape[2]
    groups = width // LANES
    steps = tokens // BLOCKS
    part = groups // halves
    half = part * LANES

    bits = [1 << n for n in range(nctx.bit_length() - 1)]
    signs = [b * (1 - 2 * lax.rem(ctx // b, 2)) for b in bits]

    def slot(i):
        place = ctx
        for b, sign in zip(bits, signs):
            place = place + lax.rem(i // b, 2) * sign
        return place

    def columns(c):
        return pl.ds(pl.multiple_of(c * width, LANES), width)

    def fetch(hbm, buf, sem, c):
        return pltpu.make_async_copy(hbm.at[:, columns(c)], buf.at[c], sem.at[c])

    def store_out(c):
        return pltpu.make_async_copy(obuf.at[c], out_hbm.at[:, columns(c)], o_sem.at[c])

    def swap(src, dst, to, send, recv, axis, other):
        return pltpu.make_async_remote_copy(
            src_ref=src, dst_ref=dst.at[to], send_sem=send.at[other], recv_sem=recv.at[to],
            device_id={axis: other}, device_id_type=MESH)

    def rate_copy(c, to):
        return swap(rate_in, rates, to, rate_send, rate_recv, "ctx", c)

    def lift_copy(c, to):
        return swap(lift_out, lifts, to, lift_send, lift_recv, "ctx", c)

    def state_copy(h, c, to):
        return swap(state_out.at[h, c], state_in.at[h], to, st_send.at[h], st_recv.at[h], "ctx", c)

    def total_copy(h, s, to):
        return swap(totals.at[h, seq], totals.at[h], to, tot_send.at[h], tot_recv.at[h], "seq", s)

    def start_copy(h, c, to):
        return swap(start_out.at[h, c], start_in.at[h], to, go_send.at[h], go_recv.at[h], "ctx", c)

    def each(count, body, first=0):
        lax.fori_loop(first, count, lambda i, x: (body(i), x)[1], 0)

    def plane(i):
        return lax.rem(seq + i + 1, nseq)

    barrier = pltpu.get_barrier_semaphore()

    @functools.partial(each, nctx - 1)
    def _(i):
        pl.semaphore_signal(barrier, inc=1, device_id={"ctx": slot(i + 1)}, device_id_type=MESH)

    @functools.partial(each, nseq - 1)
    def _(i):
        pl.semaphore_signal(barrier, inc=1, device_id={"seq": plane(i)}, device_id_type=MESH)

    @functools.partial(each, nctx)
    def _(i):
        fetch(k_hbm, kbuf, k_sem, slot(i)).start()
        fetch(v_hbm, vbuf, v_sem, slot(i)).start()

    rate = rate_in[...]
    rates[ctx] = rate
    lift_out[0:modes, :] = residue_in[...] * jnp.sqrt(minus_expm1(2.0 * rate))
    lift_out[modes:, :] = jnp.broadcast_to(gain_in[...], (lift_out.shape[0] - modes, width))
    lifts[ctx] = lift_out[...]

    pl.semaphore_wait(barrier, nctx + nseq - 2)

    @functools.partial(each, nctx - 1)
    def _(i):
        rate_copy(slot(i + 1), ctx).start()

    @functools.partial(each, nctx - 1)
    def _(i):
        lift_copy(slot(i + 1), ctx).start()

    @functools.partial(each, nctx)
    def _(i):
        fetch(q_hbm, qbuf, q_sem, slot(i)).start()

    block = lax.broadcasted_iota(jnp.int32, (BLOCKS, LANES), 0)

    def lanes(j):
        return pl.ds(pl.multiple_of(j * LANES, LANES), LANES)

    def wide(row):
        return jnp.broadcast_to(row, (BLOCKS, LANES))

    def ends(h, first, last):
        @functools.partial(each, last, first=first)
        def _(i):
            c = slot(i)

            if h == 0:
                @pl.when(i > 0)
                def _():
                    rate_copy(c, c).wait_recv()

                fetch(k_hbm, kbuf, k_sem, c).wait()
                fetch(v_hbm, vbuf, v_sem, c).wait()

            @functools.partial(each, part)
            def _(n):
                j = h * part + n
                g = c * groups + j
                product = kbuf[c, :, lanes(j)].astype(jnp.float32) * vbuf[c, :, lanes(j)].astype(jnp.float32)
                mixed[g] = product.astype(jnp.bfloat16).astype(jnp.float32)
                rate = rates[c, :, lanes(j)]
                pows[g, 0:modes, :] = jnp.exp(-rate)
                pows[g, modes:2 * modes, :] = jnp.exp(-steps * rate)
                x = [mixed[g, pl.ds(a, BLOCKS, stride=steps), :] for a in range(steps)]
                for m in range(modes):
                    p = wide(pows[g, pl.ds(m, 1), :])
                    span = wide(pows[g, pl.ds(modes + m, 1), :])
                    state = x[0]
                    for a in range(1, steps):
                        state = state * p + x[a]
                    shift = 1
                    while shift < BLOCKS:
                        moved = pltpu.roll(state, shift, 0)
                        state = state + jnp.where(block >= shift, span, 0.0) * moved
                        span = span * span
                        shift *= 2
                    carry[g, m] = jnp.where(block >= 1, pltpu.roll(state, 1, 0), 0.0)
                    state_out[h, c, pl.ds(m, 1), lanes(n)] = state[BLOCKS - 1:, :]

            @pl.when(i > 0)
            def _():
                state_copy(h, c, ctx).start()

    def inside(first, last):
        @functools.partial(each, last, first=first)
        def _(i):
            c = slot(i)

            @pl.when(i > 0)
            def _():
                lift_copy(c, c).wait_recv()

            @functools.partial(each, groups)
            def _(j):
                g = c * groups + j
                p = pows[g, 0:modes, :]
                w = lifts[c, 0:modes, lanes(j)]
                gain = lifts[c, pl.ds(modes, 1), lanes(j)]
                taps = []
                for a in range(steps):
                    tap = jnp.sum(w, axis=0, keepdims=True)
                    taps.append(wide(tap + gain if a == 0 else tap))
                    w = w * p
                x = [mixed[g, pl.ds(a, BLOCKS, stride=steps), :] for a in range(steps)]
                for a in range(steps):
                    y = taps[0] * x[a]
                    for b in range(a):
                        y = y + taps[a - b] * x[b]
                    inner[g, a] = y

    def gather_ends(h):
        state_in[h, ctx] = state_out[h, ctx]

        @functools.partial(each, nctx - 1)
        def _(i):
            state_copy(h, slot(i + 1), slot(i + 1)).wait_recv()

        decay = jnp.exp(-tokens * rate_in[:, h * half:(h + 1) * half])

        def link(s, state):
            local_start[h, s] = state
            return state * decay + state_in[h, s]

        totals[h, seq] = lax.fori_loop(0, nctx, link, jnp.zeros_like(decay))

        @functools.partial(each, nseq - 1)
        def _(i):
            total_copy(h, plane(i), seq).start()

    def send_starts(h):
        @functools.partial(each, nseq - 1)
        def _(i):
            total_copy(h, plane(i), plane(i)).wait_recv()

        rate = rate_in[:, h * half:(h + 1) * half]
        span_decay = jnp.exp(-(tokens * nctx) * rate)
        begin = lax.fori_loop(
            0, seq, lambda s, state: state * span_decay + totals[h, s], jnp.zeros_like(rate))

        @functools.partial(each, nctx)
        def _(i):
            c = slot(i)
            reach = jnp.exp(-(tokens * c).astype(jnp.float32) * rate)
            start_out[h, c] = local_start[h, c] + reach * begin

            @pl.when(i > 0)
            def _():
                start_copy(h, c, ctx).start()

        start_in[h, ctx] = start_out[h, ctx]

    far = -steps * block.astype(jnp.float32)

    def outputs(h):
        @functools.partial(each, nctx)
        def _(i):
            c = slot(i)

            @pl.when(i > 0)
            def _():
                start_copy(h, c, c).wait_recv()

            if h == 0:
                fetch(q_hbm, qbuf, q_sem, c).wait()

            @functools.partial(each, part)
            def _(n):
                j = h * part + n
                g = c * groups + j
                y = [inner[g, a] for a in range(steps)]
                for m in range(modes):
                    p = wide(pows[g, pl.ds(m, 1), :])
                    rate_m = wide(rates[c, pl.ds(m, 1), lanes(j)])
                    w = wide(lifts[c, pl.ds(m, 1), lanes(j)])
                    start = wide(start_in[h, c, pl.ds(m, 1), lanes(n)])
                    lifted = (carry[g, m] + jnp.exp(far * rate_m) * start) * (w * p)
                    for a in range(steps):
                        y[a] = y[a] + lifted
                        if a < steps - 1:
                            lifted = lifted * p
                for a in range(steps):
                    turned[pl.ds(a, BLOCKS, stride=steps), :] = y[a]
                pre = turned[...].astype(jnp.bfloat16).astype(jnp.float32)
                gated = qbuf[c, :, lanes(j)].astype(jnp.float32) * pre
                obuf[c, :, lanes(j)] = gated.astype(jnp.bfloat16)

            if h == halves - 1:
                store_out(c).start()

    ends(0, 0, nctx)
    if halves == 2:
        ends(1, 0, nctx // 2)
        gather_ends(0)
        ends(1, nctx // 2, nctx)
        inside(0, nctx // 2)
        gather_ends(1)
        send_starts(0)
        inside(nctx // 2, nctx)
        send_starts(1)
        outputs(0)
        outputs(1)
    else:
        inside(0, nctx // 4)
        gather_ends(0)
        inside(nctx // 4, nctx // 2)
        send_starts(0)
        inside(nctx // 2, nctx)
        outputs(0)

    @functools.partial(each, nctx)
    def _(i):
        store_out(slot(i)).wait()

    @functools.partial(each, nctx - 1)
    def _(i):
        c = slot(i + 1)
        rate_copy(c, ctx).wait_send()
        lift_copy(c, ctx).wait_send()
        for h in range(halves):
            state_copy(h, c, ctx).wait_send()
            start_copy(h, c, ctx).wait_send()

    @functools.partial(each, nseq - 1)
    def _(i):
        for h in range(halves):
            total_copy(h, plane(i), seq).wait_send()


def local(nctx, nseq, queries, key_proj, value_proj, decay_rate, residue, skip_gain):
    modes, width = decay_rate.shape
    tokens, channels = queries.shape
    groups = channels // LANES
    rows = -(-(modes + 1) // 8) * 8
    f32, bf16 = jnp.float32, jnp.bfloat16
    any_spec = pl.BlockSpec(memory_space=pltpu.HBM)
    piece = pltpu.VMEM((nctx, tokens, width), bf16)
    halves = 2 if (width // LANES) % 2 == 0 else 1
    state = pltpu.VMEM((halves, nctx, modes, width // halves), f32)
    sems = [pltpu.SemaphoreType.DMA((nctx,))] * 8 + [
        pltpu.SemaphoreType.DMA((halves, n)) for n in (nctx, nctx, nseq, nseq, nctx, nctx)]
    return pl.pallas_call(
        functools.partial(kernel, nctx, nseq, modes, halves),
        out_shape=jax.ShapeDtypeStruct((tokens, channels), bf16),
        in_specs=[pl.BlockSpec(memory_space=pltpu.VMEM)] * 3 + [any_spec] * 3,
        out_specs=any_spec,
        scratch_shapes=[
            pltpu.VMEM((nctx, modes, width), f32),
            pltpu.VMEM((nctx, rows, width), f32),
            pltpu.VMEM((rows, width), f32),
            piece, piece, piece, piece,
            pltpu.VMEM((groups, tokens, LANES), f32),
            pltpu.VMEM((groups, tokens // BLOCKS, BLOCKS, LANES), f32),
            pltpu.VMEM((groups, modes, BLOCKS, LANES), f32),
            pltpu.VMEM((groups, 2 * modes, LANES), f32),
            state, state, state,
            pltpu.VMEM((halves, nseq, modes, width // halves), f32),
            state, state,
            pltpu.VMEM((tokens, LANES), f32),
        ] + sems,
        compiler_params=pltpu.CompilerParams(
            collective_id=0, has_side_effects=True, vmem_limit_bytes=52 * 1024 * 1024),
        cost_estimate=pl.CostEstimate(
            flops=tokens * channels * 90, bytes_accessed=8 * tokens * channels,
            transcendentals=groups * modes * LANES * 12),
    )(decay_rate, residue, skip_gain[None], queries, key_proj, value_proj)


def solution(mesh):
    in_specs = (
        P(("seq", "ctx"), None),
        P(("seq", "ctx"), None),
        P(("seq", "ctx"), None),
        P(None, "ctx"),
        P(None, "ctx"),
        P("ctx"),
    )
    body = functools.partial(local, mesh.shape["ctx"], mesh.shape["seq"])
    return jax.shard_map(
        body, mesh=mesh, in_specs=in_specs, out_specs=P(("seq", "ctx"), None), check_vma=False)
```

time: 34 us -> 33.9 us (level)
  local copies, waits for them, and re-layouts: 2.29 us -> 3.17 us
  Pallas kernels: 31.3 us -> 30.5 us
    unnamed x1 -> x7, local copies, waits for them, and re-layouts: 2.29 us -> 3.17 us
    pallas_call x1, Pallas kernels: 31.3 us -> 30.5 us  [local(): pl.pallas_call(functools.partial(kernel, nctx, nseq, modes, halves), out_...]
where the time goes in v2:
time: 33.9 us; the launch traced here: 33.6 us
  Pallas kernels  30.5 us (90%)
  local copies, waits for them, and re-layouts  3.17 us (9%)
    pallas_call x1, Pallas kernels, local(): pl.pallas_call(functools.partial(kernel, nctx, nseq, modes, halves), out_...  30.5 us
    unnamed x7, local copies, waits for them, and re-layouts  3.17 us

profile of v2, /device:TPU:0, one launch (start us, length us, event | category | flops | bytes accessed | tf_op | source)
XLA Modules:
  0.0 33.6 jit_solution(14446311882396774273)
XLA Ops:
  0.0 0.0 copy-start
  0.0 0.8 %copy-done = f32[16,512]{1,0:T(8,128)S(1)} copy-done((f32[16,512]{1,0:T(8,128)S(1)}, f32[16,512]{1,0:T(8,128)}, u32[]{:S(2)}) %copy-start) | copy-done | bytes 32792
  0.8 0.0 copy-start.1
  0.8 0.8 %copy-done.1 = f32[16,512]{1,0:T(8,128)S(1)} copy-done((f32[16,512]{1,0:T(8,128)S(1)}, f32[16,512]{1,0:T(8,128)}, u32[]{:S(2)}) %copy-start.1) | copy-done | bytes 32792
  1.5 0.0 copy-start.2
  1.5 0.7 %copy-done.2 = f32[512]{0:T(512)S(1)} copy-done((f32[512]{0:T(512)S(1)}, f32[512]{0:T(512)}, u32[]{:S(2)}) %copy-start.2) | copy-done | bytes 2072
  2.2 30.5 %shard_map.64 = bf16[128,4096]{1,0:T(8,128)(2,1)S(1)} custom-call(f32[16,512]{1,0:T(8,128)S(1)} %copy-done, f32[16,512]{1,0:T(8,128)S(1)} %copy-done.1, f32[1,512]{1,0:T(1,128)S(1)} %bitcast.1, bf16[128,4096]{1,0:T(8,128)(2,1)} %q_hbm.1, bf16[128,4096]{1,0:T(8,128)(2,1)} %k_hbm.1, bf16[128,4096]{1,0:T(8,128)(2,1)} %v_hbm.1), custom_call_target="tpu_custom_call" | custom-call | flops 47185920 | bytes 4194304 | tf_op jit(solution)/shard_map/pallas_call | solution.py:322
  32.7 1.0 %copy.8 = bf16[128,4096]{1,0:T(8,128)(2,1)} copy(bf16[128,4096]{1,0:T(8,128)(2,1)S(1)} %shard_map.64) | data formatting | bytes 2097152
Async XLA Ops:
  0.0 0.8 %copy-start = (f32[16,512]{1,0:T(8,128)S(1)}, f32[16,512]{1,0:T(8,128)}, u32[]{:S(2)}) copy-start(f32[16,512]{1,0:T(8,128)} %rate_in.1) | copy-start | bytes 98308
  0.8 0.8 %copy-start.1 = (f32[16,512]{1,0:T(8,128)S(1)}, f32[16,512]{1,0:T(8,128)}, u32[]{:S(2)}) copy-start(f32[16,512]{1,0:T(8,128)} %residue_in.1) | copy-start | bytes 98308
  1.5 0.7 %copy-start.2 = (f32[512]{0:T(512)S(1)}, f32[512]{0:T(512)}, u32[]{:S(2)}) copy-start(f32[512]{0:T(512)} %param.11) | copy-start | bytes 6148

commit v3 on v2

--- a/solution.py
+++ b/solution.py
@@ -22,7 +22,7 @@
 def kernel(
     nctx, nseq, modes, halves, rate_in, residue_in, gain_in, q_hbm, k_hbm, v_hbm, out_hbm,
     rates, lifts, lift_out, kbuf, vbuf, qbuf, obuf, mixed, inner, carry, pows, state_out, state_in, local_start,
-    totals, start_out, start_in, turned,
+    totals, start_out, start_in, turned, to_steps, to_tokens,
     k_sem, v_sem, q_sem, o_sem, rate_send, rate_recv, lift_send, lift_recv, st_send, st_recv, tot_send, tot_recv,
     go_send, go_recv,
 ):
@@ -98,6 +98,13 @@
     lift_out[modes:, :] = jnp.broadcast_to(gain_in[...], (lift_out.shape[0] - modes, width))
     lifts[ctx] = lift_out[...]
 
+    row = lax.broadcasted_iota(jnp.int32, (tokens, tokens), 0)
+    col = lax.broadcasted_iota(jnp.int32, (tokens, tokens), 1)
+    to_steps[...] = jnp.where(
+        col == (row % BLOCKS) * steps + row // BLOCKS, 1.0, 0.0).astype(jnp.bfloat16)
+    to_tokens[...] = jnp.where(
+        row == (col % BLOCKS) * steps + col // BLOCKS, 1.0, 0.0).astype(jnp.bfloat16)
+
     pl.semaphore_wait(barrier, nctx + nseq - 2)
 
     @functools.partial(each, nctx - 1)
@@ -133,16 +140,20 @@
                 fetch(k_hbm, kbuf, k_sem, c).wait()
                 fetch(v_hbm, vbuf, v_sem, c).wait()
 
+            own = pl.ds(h * half, half)
+            product = kbuf[c, :, own] * vbuf[c, :, own]
+            ordered = jnp.dot(to_steps[...], product, preferred_element_type=jnp.float32)
+            for n in range(part):
+                mixed[c * groups + h * part + n] = ordered[:, n * LANES:(n + 1) * LANES]
+
             @functools.partial(each, part)
             def _(n):
                 j = h * part + n
                 g = c * groups + j
-                product = kbuf[c, :, lanes(j)].astype(jnp.float32) * vbuf[c, :, lanes(j)].astype(jnp.float32)
-                mixed[g] = product.astype(jnp.bfloat16).astype(jnp.float32)
                 rate = rates[c, :, lanes(j)]
                 pows[g, 0:modes, :] = jnp.exp(-rate)
                 pows[g, modes:2 * modes, :] = jnp.exp(-steps * rate)
-                x = [mixed[g, pl.ds(a, BLOCKS, stride=steps), :] for a in range(steps)]
+                x = [mixed[g, a * BLOCKS:(a + 1) * BLOCKS, :] for a in range(steps)]
                 for m in range(modes):
                     p = wide(pows[g, pl.ds(m, 1), :])
                     span = wide(pows[g, pl.ds(modes + m, 1), :])
@@ -182,7 +193,7 @@
                     tap = jnp.sum(w, axis=0, keepdims=True)
                     taps.append(wide(tap + gain if a == 0 else tap))
                     w = w * p
-                x = [mixed[g, pl.ds(a, BLOCKS, stride=steps), :] for a in range(steps)]
+                x = [mixed[g, a * BLOCKS:(a + 1) * BLOCKS, :] for a in range(steps)]
                 for a in range(steps):
                     y = taps[0] * x[a]
                     for b in range(a):
@@ -259,11 +270,11 @@
                         y[a] = y[a] + lifted
                         if a < steps - 1:
                             lifted = lifted * p
-                for a in range(steps):
-                    turned[pl.ds(a, BLOCKS, stride=steps), :] = y[a]
-                pre = turned[...].astype(jnp.bfloat16).astype(jnp.float32)
-                gated = qbuf[c, :, lanes(j)].astype(jnp.float32) * pre
-                obuf[c, :, lanes(j)] = gated.astype(jnp.bfloat16)
+                turned[:, lanes(n)] = jnp.concatenate(y, axis=0).astype(jnp.bfloat16)
+
+            pre = jnp.dot(to_tokens[...], turned[...], preferred_element_type=jnp.float32)
+            own = pl.ds(h * half, half)
+            obuf[c, :, own] = qbuf[c, :, own] * pre.astype(jnp.bfloat16)
 
             if h == halves - 1:
                 store_out(c).start()
@@ -336,10 +347,12 @@
             state, state, state,
             pltpu.VMEM((halves, nseq, modes, width // halves), f32),
             state, state,
-            pltpu.VMEM((tokens, LANES), f32),
+            pltpu.VMEM((tokens, width // halves), bf16),
+            pltpu.VMEM((tokens, tokens), bf16),
+            pltpu.VMEM((tokens, tokens), bf16),
         ] + sems,
         compiler_params=pltpu.CompilerParams(
-            collective_id=0, has_side_effects=True, vmem_limit_bytes=52 * 1024 * 1024),
+            collective_id=0, has_side_effects=True, vmem_limit_bytes=60 * 1024 * 1024),
         cost_estimate=pl.CostEstimate(
             flops=tokens * channels * 90, bytes_accessed=8 * tokens * channels,
             transcendentals=groups * modes * LANES * 12),

time: 33.9 us -> 36.3 us (1.071)
  Pallas kernels: 30.5 us -> 33.7 us
  local copies, waits for them, and re-layouts: 3.17 us -> 2.29 us
    pallas_call x1, Pallas kernels: 30.5 us -> 33.7 us  [local(): pl.pallas_call(functools.partial(kernel, nctx, nseq, modes, halves), out_...]
    unnamed x7 -> x1, local copies, waits for them, and re-layouts: 3.17 us -> 2.29 us
where the time goes in v3:
time: 36.3 us; the launch traced here: 36 us
  Pallas kernels  33.7 us (93%)
  local copies, waits for them, and re-layouts  2.29 us (6%)
    pallas_call x1, Pallas kernels, local(): pl.pallas_call(functools.partial(kernel, nctx, nseq, modes, halves), out_...  33.7 us
    unnamed x1, local copies, waits for them, and re-layouts  2.29 us

profile of v3, /device:TPU:0, one launch (start us, length us, event | category | flops | bytes accessed | tf_op | source)
XLA Modules:
  0.0 36.0 jit_solution(15387988432931747377)
XLA Ops:
  0.0 33.7 %shard_map.64 = bf16[128,4096]{1,0:T(8,128)(2,1)} custom-call(f32[16,512]{1,0:T(8,128)} %rate_in.1, f32[16,512]{1,0:T(8,128)} %residue_in.1, f32[1,512]{1,0:T(1,128)} %bitcast.1, bf16[128,4096]{1,0:T(8,128)(2,1)} %q_hbm.1, bf16[128,4096]{1,0:T(8,128)(2,1)} %k_hbm.1, bf16[128,4096]{1,0:T(8,128)(2,1)} %v_hbm.1), custom_call_target="tpu_custom_call" | custom-call | flops 47185920 | bytes 4194304 | tf_op jit(solution)/shard_map/pallas_call | solution.py:333
  33.8 2.3 %copy.8 = bf16[128,4096]{1,0:T(8,128)(2,1)} copy(bf16[128,4096]{1,0:T(8,128)(2,1)} %shard_map.64) | data formatting | bytes 2097152

commit v4 on v2

--- a/solution.py
+++ b/solution.py
@@ -137,26 +137,28 @@
             def _(n):
                 j = h * part + n
                 g = c * groups + j
-                product = kbuf[c, :, lanes(j)].astype(jnp.float32) * vbuf[c, :, lanes(j)].astype(jnp.float32)
-                mixed[g] = product.astype(jnp.bfloat16).astype(jnp.float32)
+                mixed[g] = (kbuf[c, :, lanes(j)] * vbuf[c, :, lanes(j)]).astype(jnp.float32)
                 rate = rates[c, :, lanes(j)]
                 pows[g, 0:modes, :] = jnp.exp(-rate)
                 pows[g, modes:2 * modes, :] = jnp.exp(-steps * rate)
-                x = [mixed[g, pl.ds(a, BLOCKS, stride=steps), :] for a in range(steps)]
+                p = [wide(pows[g, pl.ds(m, 1), :]) for m in range(modes)]
+                state = [mixed[g, pl.ds(0, BLOCKS, stride=steps), :]] * modes
+                for a in range(1, steps):
+                    x = mixed[g, pl.ds(a, BLOCKS, stride=steps), :]
+                    state = [state[m] * p[m] + x for m in range(modes)]
+                span = [wide(pows[g, pl.ds(modes + m, 1), :]) for m in range(modes)]
+                shift = 1
+                while shift < BLOCKS:
+                    moved = [pltpu.roll(one, shift, 0) for one in state]
+                    state = [
+                        state[m] + jnp.where(block >= shift, span[m], 0.0) * moved[m] for m in range(modes)]
+                    shift *= 2
+                    if shift < BLOCKS:
+                        span = [one * one for one in span]
+                moved = [pltpu.roll(one, 1, 0) for one in state]
                 for m in range(modes):
-                    p = wide(pows[g, pl.ds(m, 1), :])
-                    span = wide(pows[g, pl.ds(modes + m, 1), :])
-                    state = x[0]
-                    for a in range(1, steps):
-                        state = state * p + x[a]
-                    shift = 1
-                    while shift < BLOCKS:
-                        moved = pltpu.roll(state, shift, 0)
-                        state = state + jnp.where(block >= shift, span, 0.0) * moved
-                        span = span * span
-                        shift *= 2
-                    carry[g, m] = jnp.where(block >= 1, pltpu.roll(state, 1, 0), 0.0)
-                    state_out[h, c, pl.ds(m, 1), lanes(n)] = state[BLOCKS - 1:, :]
+                    carry[g, m] = jnp.where(block >= 1, moved[m], 0.0)
+                    state_out[h, c, pl.ds(m, 1), lanes(n)] = state[m][BLOCKS - 1:, :]
 
             @pl.when(i > 0)
             def _():
@@ -182,12 +184,15 @@
                     tap = jnp.sum(w, axis=0, keepdims=True)
                     taps.append(wide(tap + gain if a == 0 else tap))
                     w = w * p
-                x = [mixed[g, pl.ds(a, BLOCKS, stride=steps), :] for a in range(steps)]
+                    lifted = w if a == 0 else lifted
+                y = [taps[a] * mixed[g, pl.ds(0, BLOCKS, stride=steps), :] for a in range(steps)]
+                for b in range(1, steps):
+                    x = mixed[g, pl.ds(b, BLOCKS, stride=steps), :]
+                    for a in range(b, steps):
+                        y[a] = y[a] + taps[a - b] * x
+                pows[g, modes:2 * modes, :] = lifted
                 for a in range(steps):
-                    y = taps[0] * x[a]
-                    for b in range(a):
-                        y = y + taps[a - b] * x[b]
-                    inner[g, a] = y
+                    inner[g, a] = y[a]
 
     def gather_ends(h):
         state_in[h, ctx] = state_out[h, ctx]
@@ -248,22 +253,24 @@
             def _(n):
                 j = h * part + n
                 g = c * groups + j
-                y = [inner[g, a] for a in range(steps)]
-                for m in range(modes):
-                    p = wide(pows[g, pl.ds(m, 1), :])
-                    rate_m = wide(rates[c, pl.ds(m, 1), lanes(j)])
-                    w = wide(lifts[c, pl.ds(m, 1), lanes(j)])
-                    start = wide(start_in[h, c, pl.ds(m, 1), lanes(n)])
-                    lifted = (carry[g, m] + jnp.exp(far * rate_m) * start) * (w * p)
-                    for a in range(steps):
-                        y[a] = y[a] + lifted
-                        if a < steps - 1:
-                            lifted = lifted * p
+                begin = [
+                    jnp.exp(far * wide(rates[c, pl.ds(m, 1), lanes(j)]))
+                    * wide(start_in[h, c, pl.ds(m, 1), lanes(n)])
+                    for m in range(modes)]
+                lifted = [
+                    (carry[g, m] + begin[m]) * wide(pows[g, pl.ds(modes + m, 1), :]) for m in range(modes)]
+                p = [wide(pows[g, pl.ds(m, 1), :]) for m in range(modes)]
+                y = []
+                for a in range(steps):
+                    terms = [inner[g, a]] + lifted
+                    while len(terms) > 1:
+                        terms = [sum(terms[n:n + 2][1:], terms[n]) for n in range(0, len(terms), 2)]
+                    y += terms
+                    if a < steps - 1:
+                        lifted = [lifted[m] * p[m] for m in range(modes)]
                 for a in range(steps):
                     turned[pl.ds(a, BLOCKS, stride=steps), :] = y[a]
-                pre = turned[...].astype(jnp.bfloat16).astype(jnp.float32)
-                gated = qbuf[c, :, lanes(j)].astype(jnp.float32) * pre
-                obuf[c, :, lanes(j)] = gated.astype(jnp.bfloat16)
+                obuf[c, :, lanes(j)] = qbuf[c, :, lanes(j)] * turned[...].astype(jnp.bfloat16)
 
             if h == halves - 1:
                 store_out(c).start()
@@ -339,7 +346,7 @@
             pltpu.VMEM((tokens, LANES), f32),
         ] + sems,
         compiler_params=pltpu.CompilerParams(
-            collective_id=0, has_side_effects=True, vmem_limit_bytes=52 * 1024 * 1024),
+            collective_id=0, has_side_effects=True, vmem_limit_bytes=60 * 1024 * 1024),
         cost_estimate=pl.CostEstimate(
             flops=tokens * channels * 90, bytes_accessed=8 * tokens * channels,
             transcendentals=groups * modes * LANES * 12),

time: 33.9 us -> 33.5 us (0.988)
  local copies, waits for them, and re-layouts: 3.17 us -> 2.29 us
  Pallas kernels: 30.5 us -> 31 us
    unnamed x7 -> x1, local copies, waits for them, and re-layouts: 3.17 us -> 2.29 us
    pallas_call x1, Pallas kernels: 30.5 us -> 31 us  [local(): pl.pallas_call(functools.partial(kernel, nctx, nseq, modes, halves), out_...]
where the time goes in v4:
time: 33.5 us; the launch traced here: 33.3 us
  Pallas kernels  31 us (93%)
  local copies, waits for them, and re-layouts  2.29 us (7%)
    pallas_call x1, Pallas kernels, local(): pl.pallas_call(functools.partial(kernel, nctx, nseq, modes, halves), out_...  31 us
    unnamed x1, local copies, waits for them, and re-layouts  2.29 us

profile of v4, /device:TPU:0, one launch (start us, length us, event | category | flops | bytes accessed | tf_op | source)
XLA Modules:
  0.0 33.3 jit_solution(510527043218722141)
XLA Ops:
  0.0 31.0 %shard_map.64 = bf16[128,4096]{1,0:T(8,128)(2,1)} custom-call(f32[16,512]{1,0:T(8,128)} %rate_in.1, f32[16,512]{1,0:T(8,128)} %residue_in.1, f32[1,512]{1,0:T(1,128)} %bitcast.1, bf16[128,4096]{1,0:T(8,128)(2,1)} %q_hbm.1, bf16[128,4096]{1,0:T(8,128)(2,1)} %k_hbm.1, bf16[128,4096]{1,0:T(8,128)(2,1)} %v_hbm.1), custom_call_target="tpu_custom_call" | custom-call | flops 47185920 | bytes 4194304 | tf_op jit(solution)/shard_map/pallas_call | solution.py:329
  31.0 2.3 %copy.8 = bf16[128,4096]{1,0:T(8,128)(2,1)} copy(bf16[128,4096]{1,0:T(8,128)(2,1)} %shard_map.64) | data formatting | bytes 2097152

commit v5 on v4

--- a/solution.py
+++ b/solution.py
@@ -24,7 +24,7 @@
     rates, lifts, lift_out, kbuf, vbuf, qbuf, obuf, mixed, inner, carry, pows, state_out, state_in, local_start,
     totals, start_out, start_in, turned,
     k_sem, v_sem, q_sem, o_sem, rate_send, rate_recv, lift_send, lift_recv, st_send, st_recv, tot_send, tot_recv,
-    go_send, go_recv,
+    go_send, go_recv, rate_fwd, lift_fwd,
 ):
     ctx, seq = lax.axis_index("ctx"), lax.axis_index("seq")
     tokens, width = kbuf.shape[1], kbuf.shape[2]
@@ -62,6 +62,20 @@
     def lift_copy(c, to):
         return swap(lift_out, lifts, to, lift_send, lift_recv, "ctx", c)
 
+    def hand_on(buf, c, send, recv):
+        return pltpu.make_async_remote_copy(
+            src_ref=buf.at[c], dst_ref=buf.at[c], send_sem=send.at[c], recv_sem=recv.at[c],
+            device_id={"ctx": slot(1)}, device_id_type=MESH)
+
+    def rate_on(c):
+        return hand_on(rates, c, rate_fwd, rate_recv)
+
+    def lift_on(c):
+        return hand_on(lifts, c, lift_fwd, lift_recv)
+
+    def near(i):
+        return slot(jnp.where(i == 0, 1, 2 * i))
+
     def state_copy(h, c, to):
         return swap(state_out.at[h, c], state_in.at[h], to, st_send.at[h], st_recv.at[h], "ctx", c)
 
@@ -100,13 +114,13 @@
 
     pl.semaphore_wait(barrier, nctx + nseq - 2)
 
-    @functools.partial(each, nctx - 1)
-    def _(i):
-        rate_copy(slot(i + 1), ctx).start()
-
-    @functools.partial(each, nctx - 1)
-    def _(i):
-        lift_copy(slot(i + 1), ctx).start()
+    @functools.partial(each, nctx // 2)
+    def _(i):
+        rate_copy(near(i), ctx).start()
+
+    @functools.partial(each, nctx // 2)
+    def _(i):
+        lift_copy(near(i), ctx).start()
 
     @functools.partial(each, nctx)
     def _(i):
@@ -129,6 +143,10 @@
                 @pl.when(i > 0)
                 def _():
                     rate_copy(c, c).wait_recv()
+
+                    @pl.when(lax.rem(i, 2) == 0)
+                    def _():
+                        rate_on(c).start()
 
                 fetch(k_hbm, kbuf, k_sem, c).wait()
                 fetch(v_hbm, vbuf, v_sem, c).wait()
@@ -173,6 +191,10 @@
             def _():
                 lift_copy(c, c).wait_recv()
 
+                @pl.when(lax.rem(i, 2) == 0)
+                def _():
+                    lift_on(c).start()
+
             @functools.partial(each, groups)
             def _(j):
                 g = c * groups + j
@@ -302,11 +324,19 @@
     @functools.partial(each, nctx - 1)
     def _(i):
         c = slot(i + 1)
-        rate_copy(c, ctx).wait_send()
-        lift_copy(c, ctx).wait_send()
         for h in range(halves):
             state_copy(h, c, ctx).wait_send()
             start_copy(h, c, ctx).wait_send()
+
+    @functools.partial(each, nctx // 2)
+    def _(i):
+        rate_copy(near(i), ctx).wait_send()
+        lift_copy(near(i), ctx).wait_send()
+
+    @functools.partial(each, nctx // 2, first=1)
+    def _(i):
+        rate_on(near(i)).wait_send()
+        lift_on(near(i)).wait_send()
 
     @functools.partial(each, nseq - 1)
     def _(i):
@@ -325,7 +355,8 @@
     halves = 2 if (width // LANES) % 2 == 0 else 1
     state = pltpu.VMEM((halves, nctx, modes, width // halves), f32)
     sems = [pltpu.SemaphoreType.DMA((nctx,))] * 8 + [
-        pltpu.SemaphoreType.DMA((halves, n)) for n in (nctx, nctx, nseq, nseq, nctx, nctx)]
+        pltpu.SemaphoreType.DMA((halves, n)) for n in (nctx, nctx, nseq, nseq, nctx, nctx)] + [
+        pltpu.SemaphoreType.DMA((nctx,))] * 2
     return pl.pallas_call(
         functools.partial(kernel, nctx, nseq, modes, halves),
         out_shape=jax.ShapeDtypeStruct((tokens, channels), bf16),

time: 33.5 us -> 33 us (0.985)
  Pallas kernels: 31 us -> 30.4 us
    pallas_call x1, Pallas kernels: 31 us -> 30.4 us  [local(): pl.pallas_call(functools.partial(kernel, nctx, nseq, modes, halves), out_...]
where the time goes in v5:
time: 33 us; the launch traced here: 32.7 us
  Pallas kernels  30.4 us (92%)
  local copies, waits for them, and re-layouts  2.29 us (7%)
    pallas_call x1, Pallas kernels, local(): pl.pallas_call(functools.partial(kernel, nctx, nseq, modes, halves), out_...  30.4 us
    unnamed x1, local copies, waits for them, and re-layouts  2.29 us

profile of v5, /device:TPU:0, one launch (start us, length us, event | category | flops | bytes accessed | tf_op | source)
XLA Modules:
  0.0 32.7 jit_solution(9925732210993511965)
XLA Ops:
  0.0 30.4 %shard_map.64 = bf16[128,4096]{1,0:T(8,128)(2,1)} custom-call(f32[16,512]{1,0:T(8,128)} %rate_in.1, f32[16,512]{1,0:T(8,128)} %residue_in.1, f32[1,512]{1,0:T(1,128)} %bitcast.1, bf16[128,4096]{1,0:T(8,128)(2,1)} %q_hbm.1, bf16[128,4096]{1,0:T(8,128)(2,1)} %k_hbm.1, bf16[128,4096]{1,0:T(8,128)(2,1)} %v_hbm.1), custom_call_target="tpu_custom_call" | custom-call | flops 47185920 | bytes 4194304 | tf_op jit(solution)/shard_map/pallas_call | solution.py:360
  30.5 2.3 %copy.8 = bf16[128,4096]{1,0:T(8,128)(2,1)} copy(bf16[128,4096]{1,0:T(8,128)(2,1)} %shard_map.64) | data formatting | bytes 2097152

commit v6 on v5

--- a/solution.py
+++ b/solution.py
@@ -88,6 +88,15 @@
     def each(count, body, first=0):
         lax.fori_loop(first, count, lambda i, x: (body(i), x)[1], 0)
 
+    def pairs(count, body):
+        if count % 2:
+            each(count, body)
+        elif count == 2:
+            for n in range(2):
+                body(n)
+        else:
+            each(count // 2, lambda i: (body(2 * i), body(2 * i + 1)))
+
     def plane(i):
         return lax.rem(seq + i + 1, nseq)
 
@@ -129,7 +138,7 @@
     block = lax.broadcasted_iota(jnp.int32, (BLOCKS, LANES), 0)
 
     def lanes(j):
-        return pl.ds(pl.multiple_of(j * LANES, LANES), LANES)
+        return pl.ds(j * LANES if isinstance(j, int) else pl.multiple_of(j * LANES, LANES), LANES)
 
     def wide(row):
         return jnp.broadcast_to(row, (BLOCKS, LANES))
@@ -151,7 +160,7 @@
                 fetch(k_hbm, kbuf, k_sem, c).wait()
                 fetch(v_hbm, vbuf, v_sem, c).wait()
 
-            @functools.partial(each, part)
+            @functools.partial(pairs, part)
             def _(n):
                 j = h * part + n
                 g = c * groups + j
@@ -195,7 +204,7 @@
                 def _():
                     lift_on(c).start()
 
-            @functools.partial(each, groups)
+            @functools.partial(pairs, groups)
             def _(j):
                 g = c * groups + j
                 p = pows[g, 0:modes, :]
@@ -271,7 +280,7 @@
             if h == 0:
                 fetch(q_hbm, qbuf, q_sem, c).wait()
 
-            @functools.partial(each, part)
+            @functools.partial(pairs, part)
             def _(n):
                 j = h * part + n
                 g = c * groups + j

time: 33 us -> 32.7 us (level)
  no operation moved by 1% of the time
where the time goes in v6:
time: 32.7 us; the launch traced here: 32.5 us
  Pallas kernels  30.2 us (92%)
  local copies, waits for them, and re-layouts  2.29 us (7%)
    pallas_call x1, Pallas kernels, local(): pl.pallas_call(functools.partial(kernel, nctx, nseq, modes, halves), out_...  30.2 us
    unnamed x1, local copies, waits for them, and re-layouts  2.29 us

profile of v6, /device:TPU:0, one launch (start us, length us, event | category | flops | bytes accessed | tf_op | source)
XLA Modules:
  0.0 32.5 jit_solution(13697469866394370023)
XLA Ops:
  0.0 30.2 %shard_map.64 = bf16[128,4096]{1,0:T(8,128)(2,1)} custom-call(f32[16,512]{1,0:T(8,128)} %rate_in.1, f32[16,512]{1,0:T(8,128)} %residue_in.1, f32[1,512]{1,0:T(1,128)} %bitcast.1, bf16[128,4096]{1,0:T(8,128)(2,1)} %q_hbm.1, bf16[128,4096]{1,0:T(8,128)(2,1)} %k_hbm.1, bf16[128,4096]{1,0:T(8,128)(2,1)} %v_hbm.1), custom_call_target="tpu_custom_call" | custom-call | flops 47185920 | bytes 4194304 | tf_op jit(solution)/shard_map/pallas_call | solution.py:369
  30.2 2.3 %copy.8 = bf16[128,4096]{1,0:T(8,128)(2,1)} copy(bf16[128,4096]{1,0:T(8,128)(2,1)} %shard_map.64) | data formatting | bytes 2097152

commit v7 on v6

--- a/solution.py
+++ b/solution.py
@@ -212,8 +212,12 @@
                 gain = lifts[c, pl.ds(modes, 1), lanes(j)]
                 taps = []
                 for a in range(steps):
-                    tap = jnp.sum(w, axis=0, keepdims=True)
-                    taps.append(wide(tap + gain if a == 0 else tap))
+                    tap = sum(w[n:n + BLOCKS] for n in range(0, modes, BLOCKS))
+                    shift = BLOCKS // 2
+                    while shift:
+                        tap = tap + pltpu.roll(tap, shift, 0)
+                        shift //= 2
+                    taps.append(tap + wide(gain) if a == 0 else tap)
                     w = w * p
                     lifted = w if a == 0 else lifted
                 y = [taps[a] * mixed[g, pl.ds(0, BLOCKS, stride=steps), :] for a in range(steps)]

time: 32.7 us -> 32.7 us (level)
  no operation moved by 1% of the time
where the time goes in v7:
time: 32.7 us; the launch traced here: 32.5 us
  Pallas kernels  30.2 us (92%)
  local copies, waits for them, and re-layouts  2.29 us (7%)
    pallas_call x1, Pallas kernels, local(): pl.pallas_call(functools.partial(kernel, nctx, nseq, modes, halves), out_...  30.2 us
    unnamed x1, local copies, waits for them, and re-layouts  2.29 us

profile of v7, /device:TPU:0, one launch (start us, length us, event | category | flops | bytes accessed | tf_op | source)
XLA Modules:
  0.0 32.5 jit_solution(8723802450541168394)
XLA Ops:
  0.0 30.2 %shard_map.64 = bf16[128,4096]{1,0:T(8,128)(2,1)} custom-call(f32[16,512]{1,0:T(8,128)} %rate_in.1, f32[16,512]{1,0:T(8,128)} %residue_in.1, f32[1,512]{1,0:T(1,128)} %bitcast.1, bf16[128,4096]{1,0:T(8,128)(2,1)} %q_hbm.1, bf16[128,4096]{1,0:T(8,128)(2,1)} %k_hbm.1, bf16[128,4096]{1,0:T(8,128)(2,1)} %v_hbm.1), custom_call_target="tpu_custom_call" | custom-call | flops 47185920 | bytes 4194304 | tf_op jit(solution)/shard_map/pallas_call | solution.py:373
  30.2 2.3 %copy.8 = bf16[128,4096]{1,0:T(8,128)(2,1)} copy(bf16[128,4096]{1,0:T(8,128)(2,1)} %shard_map.64) | data formatting | bytes 2097152
